TPU v7x, 128 devices: a whole 4x4x4 slice. The times are simulated.
128 devices in a mesh: snp: 16 (over x, y_lo, core), ind: 8 (over y_hi, z).
Axes of the slice: x: 4, y: 4 (y_hi: 2, y_lo: 2; y = y_hi * 2 + y_lo), z: 4, core: 2. Of those that a mesh axis runs over, the one named last changes fastest.
Arguments:
- dosages: bfloat16 [32768, 16384], P('ind', 'snp'), may hold values from -6 to 6
- window_end: int32 [32], P('snp'), may hold values from 0 to 31, as said below
Outputs:
- ld_band: float32 [32, 5, 512, 512], P('snp', None, 'ind')
- ld_mirror: float32 [32, 5, 512, 512], P('snp', None, 'ind')
Inputs may be any that keep to these rules, and one draw needn't show every extreme that they name: window_end[i] lies between i and i + 4, and never past 32 - 1; block 0's window reaches exactly 4 blocks ahead.
All inputs are finite; a program needn't handle non-finite values.
Results may differ from a plain program's by a relative error of at most 0.0003.
Values may be sent and summed in bfloat16 or wider, within the bound.
A program may use at most 128 MiB of HBM per device.

v0:
```python
import jax
import jax.numpy as jnp
from jax import lax
from jax.sharding import PartitionSpec as P


def passed_along(value, axis, steps):
    count = lax.axis_size(axis)
    initial, last = (max(0, -steps), min(count, count - steps))
    return lax.ppermute(value, axis, [(source, source + steps) for source in range(initial, last)])


def local(dosages, window_end):
    block_count = window_end.shape[0]
    block_width = dosages.shape[1] // block_count
    offset_count = 2 * block_count + 1
    ind_groups = lax.axis_size("ind")
    ind_total = float(dosages.shape[0] * ind_groups)
    nearby = passed_along(dosages, "snp", -1)
    farther = passed_along(dosages, "snp", -2)
    sources = (dosages, nearby, farther)
    first_block = lax.axis_index("snp") * block_count

    def column_block(position):
        source = sources[position // block_count]
        column_start = position % block_count * block_width
        return source[:, column_start : column_start + block_width]

    tile_rows = []
    for local_block in range(block_count):
        left_block = column_block(local_block)
        tile_list = []
        for offset in range(offset_count):
            right_block = column_block(local_block + offset)
            is_valid = first_block + local_block + offset <= window_end[local_block]
            product = lax.dot_general(
                left_block,
                right_block,
                (((0,), (0,)), ((), ())),
                preferred_element_type=jnp.float32,
            )
            tile_value = jnp.where(is_valid, product / ind_total, jnp.float32(0.0))
            tile_list.append(tile_value)
        tile_rows.append(jnp.stack(tile_list))
    partials = jnp.stack(tile_rows)
    share = block_width // ind_groups
    rank_start = lax.axis_index("ind") * share
    totals = lax.psum(partials, "ind")
    ld_rows = lax.dynamic_slice_in_dim(totals, rank_start, share, 2)
    ld_columns = lax.dynamic_slice_in_dim(totals, rank_start, share, 3)
    turned = jnp.swapaxes(ld_columns, 2, 3)
    zero_piece = jnp.zeros((share, block_width), jnp.float32)
    outgoing = []
    for distance in range(3):
        dest_list = []
        for dest_block in range(block_count):
            piece_list = []
            for offset in range(offset_count):
                anchor = dest_block + distance * block_count - offset
                if 0 <= anchor < block_count:
                    piece_list.append(turned[anchor, offset])
                else:
                    piece_list.append(zero_piece)
            dest_list.append(jnp.stack(piece_list))
        outgoing.append(jnp.stack(dest_list))
    near_part = passed_along(outgoing[1], "snp", 1)
    far_part = passed_along(outgoing[2], "snp", 2)
    ld_mirror = outgoing[0] + near_part + far_part
    return (ld_rows, ld_mirror)


def solution(mesh):
    in_specs = (P("ind", "snp"), P("snp"))
    out_specs = (P("snp", None, "ind", None), P("snp", None, "ind", None))
    return jax.shard_map(local, mesh=mesh, in_specs=in_specs, out_specs=out_specs, check_vma=False)
```

profile of v0, /device:TPU:9, one launch (start us, length us, event | category | flops | bytes accessed | tf_op | source)
XLA Modules:
  0.0 610.6 jit_solution(12924217751028129302)
XLA Ops:
  7.2 2.6 collective-permute-start
  9.8 2.0 collective-permute-start.1
  11.8 1.3 fusion.219
  19.6 5.9 fusion.96
  25.6 2.4 fusion.87
  28.0 2.4 fusion.214
  30.3 160.7 %collective-permute-done = bf16[4096,1024]{1,0:T(8,128)(2,1)} collective-permute-done((bf16[4096,1024]{1,0:T(8,128)(2,1)}, bf16[4096,1024]{1,0:T(8,128)(2,1)}, u32[]{:S(2)}, u32[]{:S(2)}) %collective-permute-start) | collective-permute-done | bytes 8388640 | tf_op jit(solution)/shard_map/ppermute | solution.py:10
  191.0 4.5 fusion.184
  195.5 4.6 fusion.154
  200.1 4.6 fusion.124
  204.7 4.6 fusion.109
  209.2 4.7 fusion.199
  214.0 4.6 fusion.169
  218.5 4.6 fusion.139
  223.1 6.1 pad_maximum_fusion
  229.2 309.9 %all-reduce.4.cloned.1.call-done = f32[2,5,512,512]{3,2,1,0:T(8,128)} async-done(((f32[2,5,512,512]{3,2,1,0:T(8,128)}), f32[2,5,512,512]{3,2,1,0:T(8,128)}) %all-reduce.4.cloned.1.call-update) | async-done | bytes 10485776 | tf_op jit(solution)/shard_map/psum | solution.py:48
  539.1 2.5 dynamic-slice_bitcast_fusion
  541.8 2.1 fusion.79
  544.0 0.2 pad_maximum_fusion.1
  544.2 1.8 copy.5
  546.0 4.5 collective-permute-start.2
  550.5 1.9 pad_maximum_fusion.2
  552.4 1.8 copy.7
  554.3 2.2 collective-permute-start.3
  556.5 1.2 pad_bitcast_fusion.1
  557.6 2.5 constant_dynamic-slice_fusion
  560.1 13.0 %collective-permute-done.2 = f32[2,5,64,512]{3,2,1,0:T(8,128)} collective-permute-done((f32[2,5,64,512]{3,2,1,0:T(8,128)}, f32[2,5,64,512]{3,2,1,0:T(8,128)}, u32[]{:S(2)}, u32[]{:S(2)}) %collective-permute-start.2) | collective-permute-done | bytes 1310752 | tf_op jit(solution)/shard_map/ppermute | solution.py:10
  573.1 1.9 copy.6
  575.0 18.4 %collective-permute-done.3 = f32[2,5,64,512]{3,2,1,0:T(8,128)} collective-permute-done((f32[2,5,64,512]{3,2,1,0:T(8,128)}, f32[2,5,64,512]{3,2,1,0:T(8,128)}, u32[]{:S(2)}, u32[]{:S(2)}) %collective-permute-start.3) | collective-permute-done | bytes 1310752 | tf_op jit(solution)/shard_map/ppermute | solution.py:10
  593.5 3.0 copy.8
  596.5 4.4 fusion.14
  600.9 2.9 copy.9
  (8 shorter events, 0.3 us)
Async XLA Ops:
  7.2 531.9 %all-reduce.4.cloned.1.call-start = ((), (), s32[]{:S(2)}) async-start(), calls=%async_computation | async-start | bytes 20971520 | tf_op jit(solution)/shard_map/psum | solution.py:48
  7.2 183.8 %collective-permute-start = (bf16[4096,1024]{1,0:T(8,128)(2,1)}, bf16[4096,1024]{1,0:T(8,128)(2,1)}, u32[]{:S(2)}, u32[]{:S(2)}) collective-permute-start(bf16[4096,1024]{1,0:T(8,128)(2,1)} %param.2), channel_id=1, source_target_pairs={{8,0},{16,8},{24,16},{32,24},{40,32},{48,40},{56,48},{64,56},{72,6... | collective-permute-start | bytes 25165832 | tf_op jit(solution)/shard_map/ppermute | solution.py:10
  9.8 190.3 %collective-permute-start.1 = (bf16[4096,1024]{1,0:T(8,128)(2,1)}, bf16[4096,1024]{1,0:T(8,128)(2,1)}, u32[]{:S(2)}, u32[]{:S(2)}) collective-permute-start(bf16[4096,1024]{1,0:T(8,128)(2,1)} %param.2), channel_id=1, source_target_pairs={{16,0},{24,8},{32,16},{40,24},{48,32},{56,40},{64,48},{72,56},{80,... | collective-permute-start | bytes 25165832 | tf_op jit(solution)/shard_map/ppermute | solution.py:10
  19.6 6.0 copy-start
  546.0 27.1 %collective-permute-start.2 = (f32[2,5,64,512]{3,2,1,0:T(8,128)}, f32[2,5,64,512]{3,2,1,0:T(8,128)}, u32[]{:S(2)}, u32[]{:S(2)}) collective-permute-start(f32[2,5,64,512]{3,2,1,0:T(8,128)} %copy.5), channel_id=1, source_target_pairs={{0,8},{8,16},{16,24},{24,32},{32,40},{40,48},{48,56},{56,64},{64,7... | collective-permute-start | bytes 3932168 | tf_op jit(solution)/shard_map/ppermute | solution.py:10
  554.3 39.2 %collective-permute-start.3 = (f32[2,5,64,512]{3,2,1,0:T(8,128)}, f32[2,5,64,512]{3,2,1,0:T(8,128)}, u32[]{:S(2)}, u32[]{:S(2)}) collective-permute-start(f32[2,5,64,512]{3,2,1,0:T(8,128)} %copy.7), channel_id=1, source_target_pairs={{0,16},{8,24},{16,32},{24,40},{32,48},{40,56},{48,64},{56,72},{64,... | collective-permute-start | bytes 3932168 | tf_op jit(solution)/shard_map/ppermute | solution.py:10
Sparse Core Ops, SparseCore 0:
  229.3 309.7 all-reduce.3
where the time goes:
time: 613 us; the launch traced here: 611 us
  waiting for transfers between devices  502 us (82%)
  matrix products  42.7 us (7%)
  between operations  20.7 us (3%)
  local copies, waits for them, and re-layouts  19.2 us (3%)
  other arithmetic  14.7 us (2%)
  starting transfers between devices  11.3 us (2%)
    psum x1, waiting for transfers between devices, local(): totals = lax.psum(partials, 'ind')  310 us
    ppermute x4, waiting for transfers between devices, passed_along(): lax.ppermute(value, axis, [(source, source + steps) for source in range(i...  192 us
    dot_general x10, matrix products, local(): lax.dot_general(left_block, right_block, (((0,), (0,)), ((), ())), prefer...  42.7 us
  transfers between devices with their start and end apart: 5, of which 4 were waited for; matrix products, arithmetic and copies ran while one was open for 5% of the time, Pallas kernels for 0%

commit v1 on v0

v1 whole, which is shorter than its diff:
```python
import functools

import jax
import jax.numpy as jnp
from jax import lax
from jax.experimental import pallas as pl
from jax.experimental.pallas import tpu as pltpu
from jax.sharding import PartitionSpec as P

MESH = pl.DeviceIdType.MESH
F32 = jnp.float32
RANKS = 8
DEVS = 16
CHUNK = 512
AHEAD = 4


def both(condition, then, otherwise):
    pl.when(condition)(then)
    pl.when(jnp.logical_not(condition))(otherwise)


def kernel(right_blocks, left_blocks, pick_ref, x_ref, band, mirror, *refs):
    names = list(scratch(right_blocks, left_blocks))
    r = dict(zip(names, refs))
    xb, q, stage = r["xb"], r["q"], r["stage"]
    snp, ind = lax.axis_index("snp"), lax.axis_index("ind")
    odd = lax.rem(snp, 2) == 1
    even = jnp.logical_not(odd)
    parity = lax.rem(snp, 2)
    partner = snp + 1 - 2 * parity
    across = snp - 1 + 2 * parity
    has_q = jnp.logical_and(across >= 0, across < DEVS)
    across = jnp.clip(across, 0, DEVS - 1)
    hi, z = ind // 4, lax.rem(ind, 4)
    chunks = x_ref.shape[0] // CHUNK
    width = x_ref.shape[1] // 2

    loads = []
    for block in range(2):
        load = pltpu.make_async_copy(x_ref.at[:, pl.ds(block * width, width)], xb.at[block], r["load_sem"].at[block])
        load.start()
        loads.append(load)
    band[...] = jnp.zeros_like(band)
    mirror[...] = jnp.zeros_like(mirror)

    barrier = pltpu.get_barrier_semaphore()

    @pl.loop(0, RANKS)
    def _(other):
        pl.semaphore_signal(barrier, inc=1, device_id=(partner, other), device_id_type=MESH)

        @pl.when(other != ind)
        def _():
            pl.semaphore_signal(barrier, inc=1, device_id=(snp, other), device_id_type=MESH)

    @pl.when(has_q)
    def _():
        pl.semaphore_signal(barrier, inc=1, device_id=(across, ind), device_id_type=MESH)

    both(
        has_q,
        lambda: pl.semaphore_wait(barrier, 2 * RANKS),
        lambda: pl.semaphore_wait(barrier, 2 * RANKS - 1),
    )
    for load in loads:
        load.wait()

    pieces = [(n, s) for n in range(max(right_blocks, left_blocks)) for s in range(2)]

    def sends(n):
        return has_q if n < min(right_blocks, left_blocks) else jnp.logical_and(has_q, odd if right_blocks > n else even)

    def receives(n):
        return has_q if n < min(right_blocks, left_blocks) else jnp.logical_and(has_q, even if right_blocks > n else odd)

    def halo(n, s, c):
        rows = pl.ds(pl.multiple_of(c * CHUNK, CHUNK), CHUNK)
        half = jnp.where(odd, s, 1 - s)
        cols = pl.ds(pl.multiple_of(half * (width // 2), width // 2), width // 2)
        if right_blocks == 1:
            src = stage.at[rows, cols]
        else:
            src = xb.at[jnp.where(odd, 1 - n, n), rows, cols]
        at = (n * 2 + s) * chunks + c
        return pltpu.make_async_remote_copy(
            src, q.at[n, s, rows], r["halo_send"].at[at], r["halo_recv"].at[at], device_id=(across, ind), device_id_type=MESH
        )

    def start_halo(number):
        n, s, c = number // (2 * chunks), number // chunks % 2, number % chunks
        pl.when(sends(n))(lambda: halo(n, s, c).start())

    swap = [
        pltpu.make_async_remote_copy(
            xb.at[block], xb.at[2 + block], r["swap_send"].at[block], r["swap_recv"].at[block],
            device_id=(partner, ind), device_id_type=MESH,
        )
        for block in range(2)
    ]

    if right_blocks == 1:
        picked = jnp.where(odd, pick_ref[0], 0)
        for c in range(chunks):
            rows = pl.ds(c * CHUNK, CHUNK)
            stage[rows, :] = xb[picked, rows, :]
    for number in range(AHEAD):
        start_halo(number)
    for copy in swap:
        copy.start()

    def half_of(s):
        return jnp.where(odd, 1 - s, s)

    def tile(acc, s, t, a, b):
        cols = pl.ds(pl.multiple_of(half_of(s) * (width // 2), width // 2), width // 2)
        acc[s, :, t] = jnp.zeros((4, 64, width), F32)

        @pl.loop(0, xb.shape[1] // 1024)
        def _(k):
            rows = pl.ds(pl.multiple_of(k * 1024, 1024), 1024)
            product = lax.dot_general(
                xb[a, rows, cols], xb[b, rows, :], (((0,), (0,)), ((), ())), preferred_element_type=F32
            )
            acc[s, :, t] += product.reshape(4, 64, width)

    class Family:
        def __init__(self, name, number):
            self.number, self.name = number, name
            self.acc, self.zr, self.red, self.yr, self.rt, self.mt = (r[name + k] for k in ("acc", "zr", "red", "yr", "rt", "mt"))

        def z_copy(self, s, k):
            other = lax.rem(z + k, 4)
            at = self.number * 6 + s * 3 + k - 1
            return pltpu.make_async_remote_copy(
                self.acc.at[s, other], self.zr.at[s, 3 - k], r["z_send"].at[at], r["z_recv"].at[at],
                device_id=(snp, hi * 4 + other), device_id_type=MESH,
            )

        def z_start(self, s):
            for k in range(1, 4):
                self.z_copy(s, k).start()

        def y_copy(self, s):
            return pltpu.make_async_remote_copy(
                self.red.at[s], self.yr, r["y_send"].at[self.number], r["y_recv"].at[self.number],
                device_id=(snp, (1 - hi) * 4 + z), device_id_type=MESH,
            )

        def z_finish(self, s):
            for k in range(1, 4):
                self.z_copy(s, k).wait_recv()
            self.red[s] = self.acc[s, z] + self.zr[s, 0] + self.zr[s, 1] + self.zr[s, 2]
            pl.when(hi != half_of(s))(lambda: self.y_copy(s).start())

        def y_finish(self, s, packs, then):
            @pl.when(hi == half_of(s))
            def _():
                self.y_copy(s).wait_recv()
                self.yr[...] = self.yr[...] + self.red[s]
                for p, (t, u) in enumerate(packs):
                    pair = jnp.concatenate([self.yr[t], self.yr[u]], axis=0)
                    self.rt[:, p] = pair.T.reshape(RANKS, 64, 128)
                then()

        def drain(self):
            for s in range(2):
                for k in range(1, 4):
                    self.z_copy(s, k).wait_send()
            for s in range(2):
                pl.when(hi != half_of(s))(lambda: self.y_copy(s).wait_send())

        def pack_copy(self, p, kind, device, other, source):
            return pltpu.make_async_remote_copy(
                self.rt.at[other, p], self.mt.at[kind, source],
                r["pack_send"].at[(self.number * 3 + kind) * RANKS + other],
                r["pack_recv"].at[(self.number * 3 + kind) * RANKS + source],
                device_id=(device, other), device_id_type=MESH,
            )

        def pack_send(self, p, kind, to_self):
            @pl.loop(0, RANKS)
            def _(other):
                if to_self:
                    pl.when(other != ind)(lambda: self.pack_copy(p, kind, snp, other, ind).start())
                else:
                    self.pack_copy(p, kind, partner, other, ind).start()

            if to_self:
                self.mt[kind, ind] = self.rt[ind, p]

        def pack_drain(self, p, kind, to_self):
            @pl.loop(0, RANKS)
            def _(other):
                if to_self:
                    pl.when(other != ind)(lambda: self.pack_copy(p, kind, snp, other, ind).wait_send())
                else:
                    self.pack_copy(p, kind, partner, other, ind).wait_send()

        def pack_wait(self, kind, from_self):
            @pl.loop(0, RANKS)
            def _(source):
                if from_self:
                    pl.when(source != ind)(lambda: self.pack_copy(0, kind, snp, 0, source).wait_recv())
                else:
                    self.pack_copy(0, kind, partner, 0, source).wait_recv()

        def turned(self, kind, side):
            lanes = slice(64 * side, 64 * side + 64)
            return jnp.concatenate([self.mt[kind, source][:, lanes] for source in range(RANKS)], axis=1)

    inner, near = Family("i", 0), Family("a", 1)
    far = Family("b", 2) if max(right_blocks, left_blocks) == 2 else None

    def forward(at, src, dst, device):
        return pltpu.make_async_remote_copy(
            src, dst, r["fwd_send"].at[at], r["fwd_recv"].at[at], device_id=(device, ind), device_id_type=MESH
        )

    fwd_inner = lambda: forward(0, inner.yr.at[pl.ds(3, 2)], band.at[1, pl.ds(1, 2)], partner)
    fwd_even_one = lambda: forward(1, near.yr.at[0], band.at[1, 2], across)
    fwd_even_two = lambda: forward(2, near.yr.at[pl.ds(2, 2)], band.at[1, pl.ds(3, 2)], across)
    fwd_odd = lambda: forward(3, near.yr, mirror.at[0, pl.ds(1, 4)], across)
    fwd_even_far = lambda: forward(4, far.yr, band.at[0, pl.ds(3, 2)], across)
    fwd_odd_far = lambda: forward(5, far.yr.at[1], mirror.at[1, 4], across)

    def inner_places():
        band[0, 0] = inner.yr[0]
        mirror[0, 0] = inner.yr[0]
        band[1, 0] = inner.yr[1]
        mirror[1, 0] = inner.yr[1]
        band[0, 1] = inner.yr[2]
        inner.pack_send(0, 0, True)

        @pl.when(odd)
        def _():
            fwd_inner().start()
            inner.pack_send(1, 1, True)

        @pl.when(even)
        def _():
            band[0, 2] = inner.yr[3]
            band[0, 3] = inner.yr[4]
            inner.pack_send(1, 2, False)

    def near_places():
        @pl.when(odd)
        def _():
            fwd_odd().start()

        @pl.when(even)
        def _():
            fwd_even_one().start()
            fwd_even_two().start()

        near.pack_send(0, 0, True)
        near.pack_send(1, 1, False)

    def far_places():
        @pl.when(even)
        def _():
            fwd_even_far().start()
            far.pack_send(0, 0, True)

        @pl.when(odd)
        def _():
            fwd_odd_far().start()

        far.pack_send(1, 1, False)

    def inner_tiles(s, waits):
        tile(inner.acc, s, 0, 0, 0)
        tile(inner.acc, s, 1, 1, 1)
        tile(inner.acc, s, 2, 0, 1)
        for copy in waits:
            copy.wait_recv()
        tile(inner.acc, s, 3, jnp.where(odd, 3, 0), jnp.where(odd, 0, 2))
        tile(inner.acc, s, 4, jnp.where(odd, 3, 0), jnp.where(odd, 1, 3))
        inner.z_start(s)

    inner_tiles(0, swap)
    inner_tiles(1, ())

    def cross(n, s, family, slots, first, last):
        acc = family.acc
        if first == 0:
            acc[s] = jnp.zeros(acc.shape[1:], F32)

        @pl.when(receives(n))
        def _():
            @pl.loop(first, last)
            def _(c):
                halo(n, s, c).wait_recv()
                rows = pl.ds(pl.multiple_of(c * CHUNK, CHUNK), CHUNK)
                left = q[n, s, rows, :]
                for t, b in enumerate(slots):
                    product = lax.dot_general(
                        left, xb[b, rows, :], (((0,), (0,)), ((), ())), preferred_element_type=F32
                    )
                    acc[s, :, t] += product.reshape(4, 64, width)

    total = len(pieces) * chunks

    def cross_step(index, first, last):
        n, s = pieces[index]
        family = near if n == 0 else far
        slots = near_slots if n == 0 else far_slots
        for c in range(first, last):
            cross(n, s, family, slots, c, c + 1)
            number = index * chunks + c
            pl.when(sends(n))(lambda: halo(n, s, c).wait_send())
            if number + AHEAD < total:
                start_halo(number + AHEAD)
        if last == chunks:
            pl.when(receives(n))(lambda: family.z_start(s))

    near_slots = [1, 0, jnp.where(odd, 3, 2), jnp.where(odd, 2, 3)]
    far_slots = [1, jnp.where(odd, 3, 2)]
    steps = [(index, first, first + chunks // 2) for index in range(len(pieces)) for first in (0, chunks // 2)]
    for number, step in enumerate(steps):
        cross_step(*step)
        if number == 1:
            inner.z_finish(0)
        if number == 2:
            inner.y_finish(0, [(2, 2), (3, 4)], inner_places)
            inner.z_finish(1)
        if number == 3:
            inner.y_finish(1, [(2, 2), (3, 4)], inner_places)
            pl.when(has_q)(lambda: near.z_finish(0))
        if number == 4:
            pl.when(has_q)(lambda: near.y_finish(0, [(0, 1), (2, 3)], near_places))
        if number == 5:
            pl.when(has_q)(lambda: near.z_finish(1))
        if number == 6:
            pl.when(has_q)(lambda: near.y_finish(1, [(0, 1), (2, 3)], near_places))
        if number == 7:
            pl.when(receives(1))(lambda: far.z_finish(0))
    if far is None:
        @pl.when(has_q)
        def _():
            near.y_finish(0, [(0, 1), (2, 3)], near_places)
            near.z_finish(1)
            near.y_finish(1, [(0, 1), (2, 3)], near_places)
    else:
        @pl.when(receives(1))
        def _():
            far.y_finish(0, [(0, 0), (1, 1)], far_places)
            far.z_finish(1)
            far.y_finish(1, [(0, 0), (1, 1)], far_places)

    inner.pack_wait(0, True)
    mirror[1, 1] = inner.turned(0, 0)

    @pl.when(odd)
    def _():
        inner.pack_wait(1, True)
        mirror[0, 1] = inner.turned(1, 0)
        mirror[1, 2] = inner.turned(1, 1)
        inner.pack_wait(2, False)
        mirror[0, 2] = inner.turned(2, 0)
        mirror[1, 3] = inner.turned(2, 1)

    pl.when(even)(lambda: fwd_inner().wait_recv())

    @pl.when(has_q)
    def _():
        near.pack_wait(0, True)

        @pl.when(odd)
        def _():
            fwd_even_one().wait_recv()
            fwd_even_two().wait_recv()
            band[1, 1] = near.turned(0, 0)
            band[0, 2] = near.turned(0, 1)
            if right_blocks == 1:
                band[0, 3] = band[1, 2]
                band[0, 4] = band[1, 3]

        @pl.when(even)
        def _():
            fwd_odd().wait_recv()
            mirror[1, 2] = near.turned(0, 0)
            if right_blocks == 1:
                mirror[1, 3] = near.turned(0, 0)

    partner_q = jnp.where(odd, snp > 1, snp < DEVS - 2)

    @pl.when(partner_q)
    def _():
        near.pack_wait(1, False)

        @pl.when(even)
        def _():
            band[1, 3] = near.turned(1, 0)
            band[0, 4] = near.turned(1, 1)

        @pl.when(odd)
        def _():
            mirror[0, 3] = near.turned(1, 0)
            mirror[1, 4] = near.turned(1, 1)
            if right_blocks == 1:
                mirror[0, 4] = near.turned(1, 0)

    if far is not None:
        @pl.when(jnp.logical_and(has_q, odd))
        def _():
            fwd_even_far().wait_recv()

        if left_blocks == 2:
            @pl.when(jnp.logical_and(has_q, even))
            def _():
                fwd_odd_far().wait_recv()

            @pl.when(jnp.logical_and(partner_q, even))
            def _():
                far.pack_wait(1, False)
                band[1, 4] = far.turned(1, 0)

        @pl.when(jnp.logical_and(has_q, even))
        def _():
            far.pack_wait(0, True)
            mirror[1, 3] = far.turned(0, 0)

        @pl.when(jnp.logical_and(partner_q, odd))
        def _():
            far.pack_wait(1, False)
            mirror[0, 4] = far.turned(1, 0)

    for copy in swap:
        copy.wait_send()
    inner.drain()
    inner.pack_drain(0, 0, True)

    @pl.when(odd)
    def _():
        fwd_inner().wait_send()
        inner.pack_drain(1, 1, True)

    pl.when(even)(lambda: inner.pack_drain(1, 2, False))

    @pl.when(has_q)
    def _():
        near.drain()
        near.pack_drain(0, 0, True)
        near.pack_drain(1, 1, False)

        @pl.when(odd)
        def _():
            fwd_odd().wait_send()

        @pl.when(even)
        def _():
            fwd_even_one().wait_send()
            fwd_even_two().wait_send()

    if far is not None:
        @pl.when(receives(1))
        def _():
            far.drain()
            far.pack_drain(1, 1, False)

            @pl.when(even)
            def _():
                fwd_even_far().wait_send()
                far.pack_drain(0, 0, True)

            @pl.when(odd)
            def _():
                fwd_odd_far().wait_send()


def scratch(right_blocks, left_blocks):
    blocks = max(right_blocks, left_blocks)
    dma = lambda count: pltpu.SemaphoreType.DMA((count,))
    shapes = {
        "xb": pltpu.VMEM((4, 4096, 512), jnp.bfloat16),
        "q": pltpu.VMEM((blocks, 2, 4096, 256), jnp.bfloat16),
        "stage": pltpu.VMEM((4096 if right_blocks == 1 else 16, 512), jnp.bfloat16),
        "load_sem": dma(2),
        "swap_send": dma(2),
        "swap_recv": dma(2),
        "halo_send": dma(blocks * 16),
        "halo_recv": dma(blocks * 16),
        "z_send": dma(18),
        "z_recv": dma(18),
        "y_send": dma(3),
        "y_recv": dma(3),
        "pack_send": dma(72),
        "pack_recv": dma(72),
        "fwd_send": dma(6),
        "fwd_recv": dma(6),
    }
    families = [("i", 5, 3), ("a", 4, 2)] + ([("b", 2, 2)] if blocks == 2 else [])
    for name, count, kinds in families:
        shapes[name + "acc"] = pltpu.VMEM((2, 4, count, 64, 512), F32)
        shapes[name + "zr"] = pltpu.VMEM((2, 3, count, 64, 512), F32)
        shapes[name + "red"] = pltpu.VMEM((2, count, 64, 512), F32)
        shapes[name + "yr"] = pltpu.VMEM((count, 64, 512), F32)
        shapes[name + "rt"] = pltpu.VMEM((RANKS, 2, 64, 128), F32)
        shapes[name + "mt"] = pltpu.VMEM((kinds, RANKS, 64, 128), F32)
    return shapes


def tiles(right_blocks, left_blocks, pick, dosages):
    out = jax.ShapeDtypeStruct((2, 5, 64, 512), F32)
    return pl.pallas_call(
        functools.partial(kernel, right_blocks, left_blocks),
        out_shape=(out, out),
        in_specs=[pl.BlockSpec(memory_space=pltpu.SMEM), pl.BlockSpec(memory_space=pl.ANY)],
        out_specs=(pl.BlockSpec(memory_space=pltpu.VMEM),) * 2,
        scratch_shapes=list(scratch(right_blocks, left_blocks).values()),
        compiler_params=pltpu.CompilerParams(
            collective_id=right_blocks * 2 + left_blocks, has_side_effects=True, vmem_limit_bytes=62 << 20
        ),
        cost_estimate=pl.CostEstimate(flops=21_474_836_480, bytes_accessed=11_000_000, transcendentals=0),
        name=f"tiles_{right_blocks}_{left_blocks}",
    )(pick, dosages)


def local(dosages, window_end):
    windows = lax.all_gather(window_end, "snp", tiled=True)
    first = lax.axis_index("snp") * 2
    block = first + jnp.arange(2, dtype=jnp.int32)[:, None]
    offset = jnp.arange(5, dtype=jnp.int32)[None, :]
    band_valid = block + offset <= window_end[:, None]
    earlier = block - offset
    reach = jnp.sum(
        jnp.where(jnp.arange(32, dtype=jnp.int32) == earlier[..., None], windows, jnp.int32(0)), axis=-1, dtype=jnp.int32
    )
    mirror_valid = jnp.logical_and(earlier >= 0, block <= reach)
    band, mirror = tiles(2, 2, jnp.zeros((1,), jnp.int32), dosages)
    scale = jnp.float32(1.0 / 32768.0)
    band = jnp.where(band_valid[..., None, None], band * scale, jnp.float32(0.0))
    mirror = jnp.where(mirror_valid[..., None, None], mirror * scale, jnp.float32(0.0))
    return band, mirror


def solution(mesh):
    in_specs = (P("ind", "snp"), P("snp"))
    out_specs = (P("snp", None, "ind", None), P("snp", None, "ind", None))
    return jax.shard_map(local, mesh=mesh, in_specs=in_specs, out_specs=out_specs, check_vma=False)
```

time: 613 us -> 312 us (0.51)
  waiting for transfers between devices: 502 us -> 0 us
  Pallas kernels: 0 us -> 294 us
  matrix products: 42.7 us -> 0 us
  between operations: 20.7 us -> 1.32 us
  local copies, waits for them, and re-layouts: 19.2 us -> 2.32 us
  starting transfers between devices: 11.3 us -> 0 us
  other arithmetic: 14.7 us -> 4.68 us
  blocking collectives: 0 us -> 8.88 us
    psum x1 -> x0, waiting for transfers between devices: 310 us -> none  [local(): totals = lax.psum(partials, 'ind')]
    pallas_call x0 -> x1, Pallas kernels: none -> 294 us  [tiles(): pl.pallas_call(functools.partial(kernel, right_blocks, left_blocks), out_...]
    ppermute x4 -> x0, waiting for transfers between devices: 192 us -> none  [passed_along(): lax.ppermute(value, axis, [(source, source + steps) for source in range(i...]
    dot_general x10 -> x0, matrix products: 42.7 us -> none  [local(): lax.dot_general(left_block, right_block, (((0,), (0,)), ((), ())), prefer...]
    ppermute x4 -> x0, starting transfers between devices: 11.3 us -> none  [passed_along(): lax.ppermute(value, axis, [(source, source + steps) for source in range(i...]
    another operation x4 -> x0, other arithmetic: 10.3 us -> none  [the longest x1 6.09 us: local(): partials = jnp.stack(tile_rows)]
    unnamed x0 -> x1, blocking collectives: none -> 8.88 us
  transfers between devices with their start and end apart: 5 -> 0, of which waited for: 4 -> 0; matrix products, arithmetic and copies ran while one was open for 5% -> 0% of each run, Pallas kernels for 0% -> 0%
where the time goes in v1:
time: 312 us
  Pallas kernels  294 us (94%)
  blocking collectives  8.88 us (3%)
  other arithmetic  4.68 us (2%)
    pallas_call x1, Pallas kernels, tiles(): pl.pallas_call(functools.partial(kernel, right_blocks, left_blocks), out_...  294 us
    unnamed x1, blocking collectives  8.88 us

profile of v1, /device:TPU:9, one launch (start us, length us, event | category | flops | bytes accessed | tf_op | source)
XLA Modules:
  0.0 311.7 jit_solution(10750637338651055252)
XLA Ops:
  0.6 1.2 dynamic-slice
  2.6 0.9 dynamic-update-slice
  3.4 8.9 %all-reduce = s32[32]{0:T(128)S(1)} all-reduce(s32[32]{0:T(128)S(1)} %dynamic-update-slice), channel_id=1, replica_groups=mesh['snp'=16,'ind'=8] {'snp'}, use_global_device_ids=true, to_apply=%add | all-reduce | flops 32 | bytes 256
  12.3 0.2 fusion
  12.5 0.7 compare_and_fusion
  13.2 0.1 copy.5
  13.3 0.1 copy.4
  13.4 294.5 %tiles_2_2.1 = (f32[2,5,64,512]{3,2,1,0:T(8,128)}, f32[2,5,64,512]{3,2,1,0:T(8,128)}) custom-call(s32[1]{0:T(128)} %constant.4.clone.1.pick_ref, bf16[4096,1024]{1,0:T(8,128)(2,1)} %x_ref.1), custom_call_target="tpu_custom_call" | custom-call | flops 21474836480 | bytes 11000000 | tf_op jit(solution)/shard_map/tiles_2_2/pallas_call | solution.py:506
  307.9 3.8 %multiply_select_fusion = (f32[2,5,64,512]{3,2,1,0:T(8,128)}, f32[2,5,64,512]{3,2,1,0:T(8,128)}) fusion(f32[2,5,64,512]{3,2,1,0:T(8,128)} %get-tuple-element.5, pred[2,5]{1,0:T(4,128)(4,1)S(1)} %copy.5, f32[2,5,64,512]{3,2,1,0:T(8,128)} %get-tuple-element.4, pred[2,5]{1,0:T(4,128)(4,1)S(1)} %copy.4), kind=kLoop, calls=%fused_computation | loop fusion | flops 1310720 | bytes 5242900 | tf_op jit(solution)/shard_map/jit(_where)/select_n | solution.py:534
  (3 shorter events, 0.0 us)
